TPU v7x, 32 devices: a whole 2x2x4 slice. The times are simulated.
32 devices in a mesh: dp: 4 (over y, x), vocab: 8 (over z, core).
Axes of the slice: x: 2, y: 2, z: 4, core: 2. Of those that a mesh axis runs over, the one named last changes fastest.
Arguments:
- hidden_states: bfloat16 [512, 4096], P('dp', 'vocab'), may hold values from -6 to 6
- teacher_logprob: bfloat16 [512, 8192], P(('dp', 'vocab')), may hold values from -12 to -0.5
- head_weight: bfloat16 [4096, 8192], P('dp', 'vocab'), may hold values from -6 to 6
- token_ids: int32 [512], P('dp'), may hold values from 0 to 8191
- padding_mask: int32 [512], P('dp'), may hold values 0 or 1
Outputs:
- logit_grad: bfloat16 [512, 8192], P('dp', 'vocab')
- hidden_grad: float32 [512, 4096], P('dp', 'vocab')
- head_grad: bfloat16 [4096, 8192], P('dp', 'vocab')
All inputs are finite; a program needn't handle non-finite values. No bound on the sum of `padding_mask` on one device may be relied on, other than what follows from the above.
Results may differ from a plain program's by a relative error of at most 0.012.
Values may be sent and summed in bfloat16 or wider, within the bound.
A program may use at most 64 MiB of HBM per device.

v0:
```python
import jax
import jax.numpy as jnp
from jax import lax
from jax.sharding import PartitionSpec as P

anchor_weight = 0.25


def local(hidden_states, teacher_logprob, head_weight, token_ids, padding_mask):
    vocab_local = head_weight.shape[1]
    hidden_full = lax.all_gather(hidden_states, "vocab", axis=1, tiled=True)
    hidden_block = lax.all_to_all(hidden_full, "dp", split_axis=1, concat_axis=0, tiled=True)
    teacher = lax.all_to_all(teacher_logprob, "vocab", split_axis=1, concat_axis=0, tiled=True)
    head_full = lax.all_gather(head_weight, "dp", axis=0, tiled=True)
    logits = jnp.dot(hidden_full, head_full, preferred_element_type=jnp.float32)
    gap = logits - teacher.astype(jnp.float32)
    top = lax.pmax(jnp.max(logits, axis=1), "vocab")
    expo = jnp.exp(logits - top[:, None])
    total, weighted = lax.psum((jnp.sum(expo, axis=1), jnp.sum(expo * gap, axis=1)), "vocab")
    columns = lax.axis_index("vocab") * vocab_local + jnp.arange(vocab_local, dtype=jnp.int32)
    onehot = (columns[None, :] == token_ids[:, None]).astype(jnp.float32)
    prob = expo / total[:, None]
    keep = padding_mask.astype(jnp.float32)[:, None]
    logit_grad = (
        keep * (prob * (gap - (weighted / total)[:, None]) + anchor_weight * (prob - onehot))
    ).astype(jnp.bfloat16)
    head_grad = lax.dot_general(
        hidden_block,
        lax.all_gather(logit_grad, "dp", axis=0, tiled=True),
        (((0,), (0,)), ((), ())),
        preferred_element_type=jnp.float32,
    )
    feature_part = lax.dot_general(
        logit_grad, head_full, (((1,), (1,)), ((), ())), preferred_element_type=jnp.float32
    )
    hidden_grad = lax.psum_scatter(feature_part, "vocab", scatter_dimension=1, tiled=True)
    return (logit_grad, hidden_grad, head_grad.astype(jnp.bfloat16))


def solution(mesh):
    in_specs = (P("dp", "vocab"), P(("dp", "vocab"), None), P("dp", "vocab"), P("dp"), P("dp"))
    out_specs = (P("dp", "vocab"), P("dp", "vocab"), P("dp", "vocab"))
    return jax.shard_map(local, mesh=mesh, in_specs=in_specs, out_specs=out_specs, check_vma=False)
```

profile of v0, /device:TPU:6, one launch (start us, length us, event | category | flops | bytes accessed | tf_op | source)
XLA Modules:
  0.0 236.7 jit_solution(7904107378465970191)
XLA Ops:
  7.2 0.0 all-gather.4.cloned.1.call-start
  7.2 1.7 copy.12
  8.9 0.0 all-gather.4.cloned.1.call-update
  8.9 0.0 all-gather.6.cloned.1.call-start
  8.9 0.7 all-gather.6.cloned.1.call-update
  9.7 1.7 copy.18
  11.3 4.9 %all-to-all-start = ((bf16[16,8,1024]{2,0,1:T(8,128)(2,1)}), bf16[16,8,1024]{2,0,1:T(8,128)(2,1)S(1)}, u32[]{:S(2)}, u32[]{:S(2)}) async-start(bf16[16,8,1024]{2,0,1:T(8,128)(2,1)} %bitcast.22), calls=%async_computation | async-start | bytes 524288 | tf_op jit(solution)/shard_map/all_to_all | solution.py:13
  16.2 0.0 all-gather.8.cloned.1.call-start
  16.3 0.7 convert_element_type.24
  16.9 20.0 %all-gather.4.cloned.1.call-done = bf16[128,4096]{0,1:T(8,128)(2,1)} async-done(((bf16[128,512]{0,1:T(8,128)(2,1)}), bf16[128,4096]{0,1:T(8,128)(2,1)}) %all-gather.4.cloned.1.call-update) | async-done | bytes 1048592 | tf_op jit(solution)/shard_map/all_gather | solution.py:11
  36.9 88.7 %all-gather.6.cloned.1.call-done = bf16[4096,1024]{1,0:T(8,128)(2,1)} async-done(((bf16[1024,1024]{1,0:T(8,128)(2,1)}), bf16[4096,1024]{1,0:T(8,128)(2,1)}) %all-gather.6.cloned.1.call-update) | async-done | bytes 8388624 | tf_op jit(solution)/shard_map/all_gather | solution.py:14
  125.6 5.1 %fusion.1 = (f32[128]{0:T(128)S(1)}, f32[128,1024]{1,0:T(8,128)S(1)}) fusion(bf16[128,4096]{0,1:T(8,128)(2,1)} %all-gather.4.cloned.1.call-done, bf16[4096,1024]{1,0:T(8,128)(2,1)} %all-gather.6.cloned.1.call-done), kind=kOutput, calls=%fused_computation.8 | convolution fusion | flops 1073872768 | bytes 9961984 | tf_op jit(solution)/shard_map/dot_general | solution.py:15
  130.7 16.5 %pmax.7 = f32[128]{0:T(128)S(1)} all-reduce(f32[128]{0:T(128)S(1)} %get-tuple-element.16), channel_id=1, replica_groups=mesh['dp'=4,'vocab'=8] {'vocab'}, use_global_device_ids=true, to_apply=%region_1.0 | all-reduce | flops 128 | bytes 1024 | tf_op jit(solution)/shard_map/pmax | solution.py:17
  147.1 0.3 fusion
  147.4 13.6 %all-reduce = (f32[128]{0:T(128)S(1)}, f32[128]{0:T(128)S(1)}) all-reduce(f32[128]{0:T(128)S(1)} %get-tuple-element.13, f32[128]{0:T(128)S(1)} %get-tuple-element.12), channel_id=1, replica_groups=mesh['dp'=4,'vocab'=8] {'vocab'}, use_global_device_ids=true, to_apply=%region_5.0 | all-reduce | flops 256 | bytes 2048 | tf_op jit(solution)/shard_map/psum | solution.py:19
  161.0 1.1 multiply_convert_fusion
  162.1 0.0 reduce-scatter.2.cloned.1.call-start
  162.2 7.7 %fusion.2 = f32[128,4096]{1,0:T(8,128)} fusion(bf16[128,1024]{1,0:T(8,128)(2,1)} %multiply_convert_fusion, bf16[4096,1024]{1,0:T(8,128)(2,1)} %all-gather.6.cloned.1.call-done), kind=kOutput, calls=%fused_computation.9 | convolution fusion | flops 1073741824 | bytes 10747904 | tf_op jit(solution)/shard_map/dot_general | solution.py:33
  169.9 18.3 %all_to_all.32 = bf16[128,4,1024]{0,2,1:T(8,128)(2,1)S(1)} all-to-all(bf16[128,4,1024]{0,2,1:T(8,128)(2,1)S(1)} %bitcast.23), channel_id=1, replica_groups=mesh['dp'=4,'vocab'=8] {'dp'}, dimensions={1} | all-to-all | bytes 2097152 | tf_op jit(solution)/shard_map/all_to_all | solution.py:12
  188.2 0.5 copy.14
  188.8 3.4 %all-gather.8.cloned.1.call-done = bf16[512,1024]{1,0:T(8,128)(2,1)} async-done(((bf16[128,1024]{1,0:T(8,128)(2,1)}), bf16[512,1024]{1,0:T(8,128)(2,1)}) %all-gather.8.cloned.1.call-update) | async-done | bytes 1048592 | tf_op jit(solution)/shard_map/all_gather | solution.py:29
  192.2 2.5 %convert_bitcast_fusion = bf16[1024,1024]{0,1:T(8,128)(2,1)S(1)} fusion(bf16[512,1024]{1,0:T(8,128)(2,1)} %all-gather.8.cloned.1.call-done, bf16[512,1024]{1,0:T(8,128)(2,1)S(1)} %bitcast.25), kind=kOutput, calls=%fused_computation | convolution fusion | flops 1074790400 | bytes 4194304 | tf_op jit(solution)/shard_map/dot_general | solution.py:27
  194.7 2.6 %copy.15 = bf16[1024,1024]{1,0:T(8,128)(2,1)} copy(bf16[1024,1024]{0,1:T(8,128)(2,1)S(1)} %convert_bitcast_fusion) | data formatting | bytes 4194304
  197.3 32.9 %reduce-scatter.2.cloned.1.call-done = f32[128,512]{1,0:T(8,128)} async-done(((f32[128,4096]{1,0:T(8,128)}), f32[128,512]{1,0:T(8,128)}) %reduce-scatter.2.cloned.1.call-update) | async-done | bytes 262160 | tf_op jit(solution)/shard_map/reduce_scatter | solution.py:36
  (9 shorter events, 0.1 us)
Async XLA Ops:
  7.2 29.8 %all-gather.4.cloned.1.call-start = ((), (), s32[]{:S(2)}) async-start(), calls=%async_computation.3 | async-start | bytes 1179648 | tf_op jit(solution)/shard_map/all_gather | solution.py:11
  8.9 116.7 %all-gather.6.cloned.1.call-start = ((), (), s32[]{:S(2)}) async-start(), calls=%async_computation.4 | async-start | bytes 10485760 | tf_op jit(solution)/shard_map/all_gather | solution.py:14
  11.3 135.8 %all-to-all-start = ((bf16[16,8,1024]{2,0,1:T(8,128)(2,1)}), bf16[16,8,1024]{2,0,1:T(8,128)(2,1)S(1)}, u32[]{:S(2)}, u32[]{:S(2)}) async-start(bf16[16,8,1024]{2,0,1:T(8,128)(2,1)} %bitcast.22), calls=%async_computation | async-start | bytes 524288 | tf_op jit(solution)/shard_map/all_to_all | solution.py:13
  16.2 176.0 %all-gather.8.cloned.1.call-start = ((), (), s32[]{:S(2)}) async-start(), calls=%async_computation.6 | async-start | bytes 1310720 | tf_op jit(solution)/shard_map/all_gather | solution.py:29
  16.9 144.1 %copy-start.1 = (s32[128]{0:T(128)S(1)}, s32[128]{0:T(128)}, u32[]{:S(2)}) copy-start(s32[128]{0:T(128)} %param.8) | copy-start | bytes 1540
  130.6 39.2 %copy-start = (bf16[128,4096]{0,1:T(8,128)(2,1)S(1)}, bf16[128,4096]{0,1:T(8,128)(2,1)}, u32[]{:S(2)}) copy-start(bf16[128,4096]{0,1:T(8,128)(2,1)} %all-gather.4.cloned.1.call-done) | copy-start | bytes 3145732
  162.1 68.0 %reduce-scatter.2.cloned.1.call-start = ((), (), s32[]{:S(2)}) async-start(), calls=%async_computation.5 | async-start | bytes 2359296 | tf_op jit(solution)/shard_map/reduce_scatter | solution.py:36
Sparse Core Ops, SparseCore 0:
  10.2 26.7 all-gather.3
  38.8 86.7 all-gather.5
  162.2 29.9 all-gather.7
  194.9 35.1 reduce-scatter.1
where the time goes:
time: 239 us; the launch traced here: 237 us
  waiting for transfers between devices  146 us (61%)
  blocking collectives  48.4 us (20%)
  matrix products  15.3 us (6%)
  between operations  13.8 us (6%)
  local copies, waits for them, and re-layouts  6.43 us (3%)
  starting transfers between devices  5.04 us (2%)
    all_gather x1, waiting for transfers between devices, local(): head_full = lax.all_gather(head_weight, 'dp', axis=0, tiled=True)  88.7 us
    reduce_scatter x1, waiting for transfers between devices, local(): lax.psum_scatter(feature_part, 'vocab', scatter_dimension=1, tiled=True)  32.9 us
    all_gather x1, waiting for transfers between devices, local(): hidden_full = lax.all_gather(hidden_states, 'vocab', axis=1, tiled=True)  20 us
    all_to_all x1, blocking collectives, local(): lax.all_to_all(hidden_full, 'dp', split_axis=1, concat_axis=0, tiled=True)  18.3 us
    pmax x1, blocking collectives, local(): top = lax.pmax(jnp.max(logits, axis=1), 'vocab')  16.5 us
    psum x1, blocking collectives, local(): lax.psum((jnp.sum(expo, axis=1), jnp.sum(expo * gap, axis=1)), 'vocab')  13.6 us
    dot_general x1, matrix products, local(): lax.dot_general(logit_grad, head_full, (((1,), (1,)), ((), ())), preferre...  7.71 us
    dot_general x1, matrix products, local(): logits = jnp.dot(hidden_full, head_full, preferred_element_type=jnp.float32)  5.07 us
  transfers between devices with their start and end apart: 5, of which 4 were waited for; matrix products, arithmetic and copies ran while one was open for 9% of the time, Pallas kernels for 0%

commit v1 on v0

v1 whole, which is shorter than its diff:
```python
import functools
import jax
import jax.numpy as jnp
from jax import lax
from jax.experimental import pallas as pl
from jax.experimental.pallas import tpu as pltpu
from jax.sharding import PartitionSpec as P

anchor_weight = 0.25
MESH = pl.DeviceIdType.MESH
F32 = jnp.float32
BF16 = jnp.bfloat16


def kernel(
    hid_ref, tea_ref, head_ref, ids_ref, mask_ref,
    lg_out, hg_out, wg_out,
    head_v, zbuf, hblk, hid_t, tea_v, part, relay, got, logits_v, stat_v, lgb,
    hown, sib_out, sib_in, d1_out, d1_in, d2_in, wg_v, hg_v,
    loc_sem, a1s, a1r, a2s, a2r, a3s, a3r, ts, tr, bs, br, ss, sr, cs, cr,
    es, er, d1s, d1r, d2s, d2r, wsem,
):
    tok, feat = hid_ref.shape
    width, voc = head_ref.shape
    half = tok // 2
    trow = tea_ref.shape[0]
    i, j = lax.axis_index("dp"), lax.axis_index("vocab")
    z, c = j // 2, j % 2
    sib = z * 2 + (1 - c)
    nx = i + 1 - 2 * (i % 2)
    ny = (i + 2) % 4
    nd = 3 - i
    rel = (i, nx, ny, nd)

    def remote(src, dst, ssem, rsem, to):
        return pltpu.make_async_remote_copy(
            src_ref=src, dst_ref=dst, send_sem=ssem, recv_sem=rsem,
            device_id=to, device_id_type=MESH,
        )

    def rows(block, start=0, size=None):
        size = tok if size is None else size
        return pl.ds(pl.multiple_of(block * tok + start, 16), size)

    mine = pl.ds(pl.multiple_of(c * feat, feat), feat)
    other = pl.ds(pl.multiple_of((1 - c) * feat, feat), feat)

    cp_hid = pltpu.make_async_copy(hid_ref, zbuf.at[z], loc_sem.at[0])
    cp_head = pltpu.make_async_copy(head_ref, head_v, loc_sem.at[1])
    own_cols = pl.ds(pl.multiple_of(j * voc, voc), voc)
    own_trow = pl.ds(pl.multiple_of(j * trow, trow), trow)
    cp_tea = pltpu.make_async_copy(tea_ref.at[:, own_cols], tea_v.at[own_trow, :], loc_sem.at[2])
    cp_hid.start()
    cp_head.start()
    cp_tea.start()

    barrier = pltpu.get_barrier_semaphore()
    for k in range(1, 4):
        pl.semaphore_signal(barrier, inc=1, device_id={"dp": (i + k) % 4}, device_id_type=MESH)
    for k in range(1, 8):
        pl.semaphore_signal(barrier, inc=1, device_id={"vocab": (j + k) % 8}, device_id_type=MESH)
    pl.semaphore_wait(barrier, 10)

    a1 = []
    for k in range(1, 4):
        cp = remote(hid_ref, zbuf.at[z], a1s.at[k], a1r.at[k], {"vocab": ((z + k) % 4) * 2 + c})
        cp.start()
        a1.append(cp)
    cp_hid.wait()

    def a2_copy(zs, shift):
        return remote(
            zbuf.at[zs], hblk.at[rows(i), mine], a2s.at[shift], a2r.at[shift], {"dp": zs}
        )

    def a2_local(zs):
        return pltpu.make_async_copy(zbuf.at[zs], hblk.at[rows(i), mine], loc_sem.at[3])

    def forward(zs):
        shift = (zs - i + 4) % 4

        @pl.when(shift != 0)
        def _():
            a2_copy(zs, shift).start()

        @pl.when(shift == 0)
        def _():
            a2_local(zs).start()

    forward(z)
    for k in range(1, 4):
        a1[k - 1].wait_recv()
        forward((z - k + 4) % 4)

    tcps = []
    for k in range(1, 8):
        jt = (j + k) % 8
        cp = remote(
            tea_ref.at[:, pl.ds(pl.multiple_of(jt * voc, voc), voc)], tea_v.at[own_trow, :],
            ts.at[k], tr.at[k], {"vocab": jt},
        )
        cp.start()
        tcps.append(cp)

    a3 = []
    for k in range(4):
        src = (i - k + 4) % 4
        if k == 0:
            a2_local(i).wait()
        else:
            a2_copy((i + k) % 4, k).wait_recv()
        piece = hblk.at[rows(src), mine]
        cp = remote(piece, piece, a3s.at[k], a3r.at[k], {"vocab": sib})
        cp.start()
        a3.append(cp)
    cp_head.wait()
    for cp in a3:
        cp.wait_recv()

    def partial_logits(r):
        x = hblk[rows(rel[r]), :]

        @pl.loop(0, voc // 256)
        def _(t):
            col = pl.ds(pl.multiple_of(t * 256, 256), 256)
            part[r, :, col] = jnp.dot(x, head_v[:, col], preferred_element_type=F32)

    lo, hi = pl.ds(0, half), pl.ds(half, half)
    to_x, to_y, to_d = {"dp": nx}, {"dp": ny}, {"dp": nd}
    b = []

    def send_b(src, dst, to):
        n = len(b)
        cp = remote(src, dst, bs.at[n], br.at[n], to)
        cp.start()
        b.append(cp)

    partial_logits(3)
    send_b(part.at[3, lo, :], relay.at[0], to_x)
    send_b(part.at[3, hi, :], relay.at[1], to_y)
    partial_logits(1)
    send_b(part.at[1, lo, :], got.at[0, lo, :], to_x)
    partial_logits(2)
    send_b(part.at[2, hi, :], got.at[1, hi, :], to_y)
    partial_logits(0)

    @pl.loop(0, width // 256)
    def _(t):
        cut = pl.ds(pl.multiple_of(t * 256, 256), 256)
        hid_t[cut, :] = jnp.swapaxes(hblk[:, cut], 0, 1)

    b[0].wait_recv()
    part[2, lo, :] = part[2, lo, :] + relay[0]
    send_b(part.at[2, lo, :], got.at[1, lo, :], to_y)
    b[1].wait_recv()
    part[1, hi, :] = part[1, hi, :] + relay[1]
    send_b(part.at[1, hi, :], got.at[0, hi, :], to_x)

    cp_tea.wait()
    for cp in tcps:
        cp.wait_recv()
    for n in (2, 3, 4, 5):
        b[n].wait_recv()

    logits = part[0] + got[0] + got[1]
    logits_v[...] = logits
    m = jnp.max(logits, axis=1, keepdims=True)
    e = jnp.exp(logits - m)
    s = jnp.sum(e, axis=1, keepdims=True)
    w = jnp.sum(e * (logits - tea_v[...].astype(F32)), axis=1, keepdims=True)
    lane = lax.broadcasted_iota(jnp.int32, (tok, tok), 1)
    packed = jnp.where(lane == 0, m, jnp.where(lane == 1, s, w))
    stat_v[j] = jnp.swapaxes(packed, 0, 1)[0:8, :]
    scps = []
    for k in range(1, 8):
        cp = remote(stat_v.at[j], stat_v.at[j], ss.at[k], sr.at[k], {"vocab": (j + k) % 8})
        cp.start()
        scps.append(cp)
    for cp in scps:
        cp.wait_recv()
    stats = stat_v[...]
    tops = stats[:, 0, :]
    top = jnp.max(tops, axis=0, keepdims=True)
    scale = jnp.exp(tops - top)
    total = jnp.sum(stats[:, 1, :] * scale, axis=0, keepdims=True)
    weighted = jnp.sum(stats[:, 2, :] * scale, axis=0, keepdims=True)
    sub = lax.broadcasted_iota(jnp.int32, (tok, tok), 0)
    table = jnp.where(sub == 0, top, jnp.where(sub == 1, total, jnp.where(
        sub == 2, weighted / total, jnp.where(
            sub == 3, ids_ref[...].astype(F32), mask_ref[...].astype(F32)))))
    table = jnp.swapaxes(table, 0, 1)
    logits = logits_v[...]
    prob = jnp.exp(logits - table[:, 0:1]) / table[:, 1:2]
    gap = logits - tea_v[...].astype(F32)
    ids = table[:, 3:4].astype(jnp.int32) - j * voc
    onehot = (lax.broadcasted_iota(jnp.int32, (tok, voc), 1) == ids).astype(F32)
    lg = table[:, 4:5] * (prob * (gap - table[:, 2:3]) + anchor_weight * (prob - onehot))
    lgb[rows(i), :] = lg.astype(BF16)

    cc = []

    def send_c(block, start, to):
        n = len(cc)
        piece = lgb.at[rows(block, start, half), :]
        cp = remote(piece, piece, cs.at[n], cr.at[n], to)
        cp.start()
        cc.append(cp)

    send_c(i, 0, to_x)
    send_c(i, half, to_y)
    send_c(i, half, to_x)
    send_c(i, 0, to_y)
    cp_lg = pltpu.make_async_copy(lgb.at[rows(i), :], lg_out, wsem.at[4])
    cp_lg.start()

    nt = (((1,), (1,)), ((), ()))
    ecps = []

    def hidden_part(r):
        g = lgb[rows(rel[r]), :]
        sib_out[r] = lax.dot_general(
            g, head_v[other, :], nt, preferred_element_type=F32).astype(BF16)
        cp = remote(sib_out.at[r], sib_in.at[r], es.at[r], er.at[r], {"vocab": sib})
        cp.start()
        ecps.append(cp)
        hown[r] = lax.dot_general(g, head_v[mine, :], nt, preferred_element_type=F32)

    hidden_part(0)
    cc[0].wait_recv()
    send_c(nx, 0, to_y)
    cc[1].wait_recv()
    send_c(ny, half, to_x)

    d1 = [None]

    def d2_copy(r, shift, zt):
        src = d1_in.at[r]
        return remote(src, d2_in.at[shift], d2s.at[shift], d2r.at[shift], {"vocab": zt * 2 + c})

    def d2_send(r):
        zt = rel[r]
        shift = (zt - z + 4) % 4

        @pl.when(shift != 0)
        def _():
            d2_copy(r, shift, zt).start()

        @pl.when(shift == 0)
        def _():
            d2_in[0] = d1_in[r]

    def reduced(r):
        ecps[r].wait_recv()
        summed = (hown[r] + sib_in[r].astype(F32)).astype(BF16)
        if r == 0:
            d1_in[0] = summed
            d2_send(0)
        else:
            d1_out[r] = summed
            cp = remote(d1_out.at[r], d1_in.at[r], d1s.at[r], d1r.at[r], (None, to_x, to_y, to_d)[r])
            cp.start()
            d1.append(cp)

    reduced(0)
    cc[2].wait_recv()
    hidden_part(1)
    cc[3].wait_recv()
    hidden_part(2)
    reduced(1)
    reduced(2)
    cc[4].wait_recv()
    cc[5].wait_recv()
    hidden_part(3)
    d1[1].wait_recv()
    d2_send(1)
    d1[2].wait_recv()
    d2_send(2)
    reduced(3)

    wcps = []
    quarter = width // 4

    def weight_part(t):
        cut = pl.ds(t * quarter, quarter)

        @pl.loop(0, voc // 256)
        def _(u):
            col = pl.ds(pl.multiple_of(u * 256, 256), 256)
            wg_v[cut, col] = jnp.dot(
                hid_t[cut, :], lgb[:, col], preferred_element_type=F32).astype(BF16)

        cp = pltpu.make_async_copy(wg_v.at[cut, :], wg_out.at[cut, :], wsem.at[t])
        cp.start()
        wcps.append(cp)

    weight_part(0)
    weight_part(1)
    d1[3].wait_recv()
    d2_send(3)
    weight_part(2)
    weight_part(3)

    for k in range(1, 4):
        d2_copy(0, k, (z + k) % 4).wait_recv()
    acc = d2_in[0].astype(F32)
    for k in range(1, 4):
        acc = acc + d2_in[k].astype(F32)
    hg_v[...] = acc
    cp_hg = pltpu.make_async_copy(hg_v, hg_out, wsem.at[5])
    cp_hg.start()

    for cp in a1 + tcps + a3 + b + scps + cc + ecps + d1[1:]:
        cp.wait_send()
    for k in range(1, 4):
        a2_copy((i + k) % 4, k).wait_send()
        d2_copy(0, k, (z + k) % 4).wait_send()
    for cp in wcps:
        cp.wait()
    cp_lg.wait()
    cp_hg.wait()


def fused(hidden_states, teacher_logprob, head_weight, token_ids, padding_mask):
    tok, feat = hidden_states.shape
    width, voc = head_weight.shape
    trow = teacher_logprob.shape[0]
    half = tok // 2
    any_spec = pl.BlockSpec(memory_space=pl.ANY)
    vmem_spec = pl.BlockSpec(memory_space=pltpu.VMEM)
    dma = pltpu.SemaphoreType.DMA
    return pl.pallas_call(
        kernel,
        out_shape=(
            jax.ShapeDtypeStruct((tok, voc), BF16),
            jax.ShapeDtypeStruct((tok, feat), F32),
            jax.ShapeDtypeStruct((width, voc), BF16),
        ),
        in_specs=[any_spec, any_spec, any_spec, vmem_spec, vmem_spec],
        out_specs=[any_spec] * 3,
        scratch_shapes=[
            pltpu.VMEM((width, voc), BF16),
            pltpu.VMEM((4, tok, feat), BF16),
            pltpu.VMEM((4 * tok, width), BF16),
            pltpu.VMEM((width, 4 * tok), BF16),
            pltpu.VMEM((8 * trow, voc), BF16),
            pltpu.VMEM((4, tok, voc), F32),
            pltpu.VMEM((2, half, voc), F32),
            pltpu.VMEM((2, tok, voc), F32),
            pltpu.VMEM((tok, voc), F32),
            pltpu.VMEM((8, 8, tok), F32),
            pltpu.VMEM((4 * tok, voc), BF16),
            pltpu.VMEM((4, tok, feat), F32),
            pltpu.VMEM((4, tok, feat), BF16),
            pltpu.VMEM((4, tok, feat), BF16),
            pltpu.VMEM((4, tok, feat), BF16),
            pltpu.VMEM((4, tok, feat), BF16),
            pltpu.VMEM((4, tok, feat), BF16),
            pltpu.VMEM((width, voc), BF16),
            pltpu.VMEM((tok, feat), F32),
            dma((4,)), dma((4,)), dma((4,)), dma((4,)), dma((4,)), dma((4,)), dma((4,)),
            dma((8,)), dma((8,)), dma((6,)), dma((6,)), dma((8,)), dma((8,)),
            dma((6,)), dma((6,)), dma((4,)), dma((4,)), dma((4,)), dma((4,)),
            dma((4,)), dma((4,)), dma((6,)),
        ],
        compiler_params=pltpu.CompilerParams(
            collective_id=0, has_side_effects=True, vmem_limit_bytes=40 * 1024 * 1024
        ),
        cost_estimate=pl.CostEstimate(
            flops=6 * 4 * tok * width * voc, bytes_accessed=6 * width * voc,
            transcendentals=2 * tok * voc,
        ),
    )(
        hidden_states, teacher_logprob, head_weight,
        token_ids.reshape(1, tok), padding_mask.reshape(1, tok),
    )


def gathered(n_dp, n_vocab, hidden_states, teacher_logprob, head_weight, token_ids, padding_mask):
    voc = head_weight.shape[1]
    full = lax.all_gather(hidden_states, "vocab", axis=1, tiled=True)
    block = lax.all_to_all(full, "dp", split_axis=1, concat_axis=0, tiled=True)
    teacher = lax.all_to_all(teacher_logprob, "vocab", split_axis=1, concat_axis=0, tiled=True)
    part = jnp.dot(block, head_weight, preferred_element_type=F32)
    logits = lax.psum_scatter(part, "dp", scatter_dimension=0, tiled=True)
    gap = logits - teacher.astype(F32)
    top = lax.pmax(jnp.max(logits, axis=1), "vocab")
    expo = jnp.exp(logits - top[:, None])
    total, weighted = lax.psum((jnp.sum(expo, axis=1), jnp.sum(expo * gap, axis=1)), "vocab")
    columns = lax.axis_index("vocab") * voc + jnp.arange(voc, dtype=jnp.int32)
    onehot = (columns[None, :] == token_ids[:, None]).astype(F32)
    prob = expo / total[:, None]
    keep = padding_mask.astype(F32)[:, None]
    logit_grad = (
        keep * (prob * (gap - (weighted / total)[:, None]) + anchor_weight * (prob - onehot))
    ).astype(BF16)
    every = lax.all_gather(logit_grad, "dp", axis=0, tiled=True)
    head_grad = lax.dot_general(
        block, every, (((0,), (0,)), ((), ())), preferred_element_type=F32).astype(BF16)
    back = lax.dot_general(
        every, head_weight, (((1,), (1,)), ((), ())), preferred_element_type=F32)
    back = lax.all_to_all(back, "dp", split_axis=0, concat_axis=1, tiled=True)
    hidden_grad = lax.psum_scatter(back, "vocab", scatter_dimension=1, tiled=True)
    return (logit_grad, hidden_grad, head_grad)


def solution(mesh):
    in_specs = (P("dp", "vocab"), P(("dp", "vocab"), None), P("dp", "vocab"), P("dp"), P("dp"))
    out_specs = (P("dp", "vocab"), P("dp", "vocab"), P("dp", "vocab"))
    n_dp, n_vocab = mesh.shape["dp"], mesh.shape["vocab"]
    body = fused if (n_dp, n_vocab) == (4, 8) else functools.partial(gathered, n_dp, n_vocab)
    return jax.shard_map(body, mesh=mesh, in_specs=in_specs, out_specs=out_specs, check_vma=False)
```

time: 239 us -> 88.8 us (0.37)
  waiting for transfers between devices: 146 us -> 0 us
  Pallas kernels: 0 us -> 79.9 us
  blocking collectives: 48.4 us -> 0 us
  matrix products: 15.3 us -> 0 us
  between operations: 13.8 us -> 0.65 us
  starting transfers between devices: 5.04 us -> 0 us
    all_gather x3 -> x0, waiting for transfers between devices: 112 us -> none  [the longest x1 88.7 us: local(): head_full = lax.all_gather(head_weight, 'dp', axis=0, tiled=True)]
    pallas_call x0 -> x1, Pallas kernels: none -> 79.9 us  [fused(): pl.pallas_call(kernel, out_shape=(jax.ShapeDtypeStruct((tok, voc), BF16),...]
    reduce_scatter x1 -> x0, waiting for transfers between devices: 32.9 us -> none  [local(): lax.psum_scatter(feature_part, 'vocab', scatter_dimension=1, tiled=True)]
    all_to_all x1 -> x0, blocking collectives: 18.3 us -> none  [local(): lax.all_to_all(hidden_full, 'dp', split_axis=1, concat_axis=0, tiled=True)]
    pmax x1 -> x0, blocking collectives: 16.5 us -> none  [local(): top = lax.pmax(jnp.max(logits, axis=1), 'vocab')]
    dot_general x3 -> x0, matrix products: 15.3 us -> none  [the longest x1 7.71 us: local(): lax.dot_general(logit_grad, head_full, (((1,), (1,)), ((), ())), preferre...]
    psum x1 -> x0, blocking collectives: 13.6 us -> none  [local(): lax.psum((jnp.sum(expo, axis=1), jnp.sum(expo * gap, axis=1)), 'vocab')]
    all_to_all x1 -> x0, starting transfers between devices: 4.88 us -> none  [local(): lax.all_to_all(teacher_logprob, 'vocab', split_axis=1, concat_axis=0, til...]
  transfers between devices with their start and end apart: 5 -> 0, of which waited for: 4 -> 0; matrix products, arithmetic and copies ran while one was open for 9% -> 0% of each run, Pallas kernels for 0% -> 0%
where the time goes in v1:
time: 88.8 us; the launch traced here: 88.1 us
  Pallas kernels  79.9 us (90%)
  local copies, waits for them, and re-layouts  7.47 us (8%)
    pallas_call x1, Pallas kernels, fused(): pl.pallas_call(kernel, out_shape=(jax.ShapeDtypeStruct((tok, voc), BF16),...  79.9 us
    unnamed x13, local copies, waits for them, and re-layouts  7.47 us

profile of v1, /device:TPU:6, one launch (start us, length us, event | category | flops | bytes accessed | tf_op | source)
XLA Modules:
  0.0 88.1 jit_solution(15356975024560283469)
XLA Ops:
  0.6 0.0 copy-start
  0.6 1.6 %copy-done = bf16[1024,1024]{1,0:T(8,128)(2,1)S(1)} copy-done((bf16[1024,1024]{1,0:T(8,128)(2,1)S(1)}, bf16[1024,1024]{1,0:T(8,128)(2,1)}, u32[]{:S(2)}) %copy-start) | copy-done | bytes 2097176
  2.2 0.0 copy-start.1
  2.2 0.9 %copy-done.1 = bf16[16,8192]{1,0:T(8,128)(2,1)S(1)} copy-done((bf16[16,8192]{1,0:T(8,128)(2,1)S(1)}, bf16[16,8192]{1,0:T(8,128)(2,1)}, u32[]{:S(2)}) %copy-start.1) | copy-done | bytes 262168
  3.2 0.0 copy-start.2
  3.2 0.9 %copy-done.2 = bf16[128,512]{1,0:T(8,128)(2,1)S(1)} copy-done((bf16[128,512]{1,0:T(8,128)(2,1)S(1)}, bf16[128,512]{1,0:T(8,128)(2,1)}, u32[]{:S(2)}) %copy-start.2) | copy-done | bytes 131096
  4.1 0.0 copy-start.3
  4.1 0.7 copy-done.3
  4.7 0.0 copy-start.4
  4.7 0.7 copy-done.4
  5.4 79.9 %shard_map.76 = (bf16[128,1024]{1,0:T(8,128)(2,1)S(1)}, f32[128,512]{1,0:T(8,128)S(1)}, bf16[1024,1024]{1,0:T(8,128)(2,1)S(1)}) custom-call(bf16[128,512]{1,0:T(8,128)(2,1)S(1)} %copy-done.2, bf16[16,8192]{1,0:T(8,128)(2,1)S(1)} %copy-done.1, bf16[1024,1024]{1,0:T(8,128)(2,1)S(1)} %copy-done, s32[1,128]{1,0:T(1,128)S(1)} %bitcast.2, s32[1,128]{1,0:T(1,128)S(1)} %bitcast.3), custom_call_target="tpu_custom_call" | custom-call | flops 3221225472 | bytes 6291456 | tf_op jit(solution)/shard_map/pallas_call | solution.py:331
  85.3 0.7 copy.11
  86.0 0.7 copy.12
  86.7 1.3 %copy.13 = bf16[1024,1024]{1,0:T(8,128)(2,1)} copy(bf16[1024,1024]{1,0:T(8,128)(2,1)S(1)} %get-tuple-element.8) | data formatting | bytes 4194304
Async XLA Ops:
  0.6 1.6 %copy-start = (bf16[1024,1024]{1,0:T(8,128)(2,1)S(1)}, bf16[1024,1024]{1,0:T(8,128)(2,1)}, u32[]{:S(2)}) copy-start(bf16[1024,1024]{1,0:T(8,128)(2,1)} %head_ref.1) | copy-start | bytes 6291460
  2.2 0.9 %copy-start.1 = (bf16[16,8192]{1,0:T(8,128)(2,1)S(1)}, bf16[16,8192]{1,0:T(8,128)(2,1)}, u32[]{:S(2)}) copy-start(bf16[16,8192]{1,0:T(8,128)(2,1)} %tea_ref.1) | copy-start | bytes 786436
  3.2 0.9 %copy-start.2 = (bf16[128,512]{1,0:T(8,128)(2,1)S(1)}, bf16[128,512]{1,0:T(8,128)(2,1)}, u32[]{:S(2)}) copy-start(bf16[128,512]{1,0:T(8,128)(2,1)} %hid_ref.1) | copy-start | bytes 393220
  4.1 0.7 copy-start.3
  4.7 0.7 copy-start.4

commit v2 on v0

v2 whole, which is shorter than its diff:
```python
import functools
import jax
import jax.numpy as jnp
from jax import lax
from jax.experimental import pallas as pl
from jax.experimental.pallas import tpu as pltpu
from jax.sharding import PartitionSpec as P

anchor_weight = 0.25
MESH = pl.DeviceIdType.MESH
F32 = jnp.float32
BF16 = jnp.bfloat16


def kernel(
    hid_ref, tea_ref, head_ref, ids_ref, mask_ref,
    lg_out, hg_out, wg_out,
    head_v, head_t, zbuf, hblk, hid_t, tea_v, ids_v, mask_v, part, relay, got, logits_v, stat_v,
    lgb, hown, sib_out, sib_in, d1_out, d1_in, d2_in, wg_v, hg_v,
    loc_sem, a1s, a1r, a2s, a2r, a3s, a3r, ts, tr, bs, br, ss, sr, cs, cr,
    es, er, d1s, d1r, d2s, d2r, wsem,
):
    tok, feat = hid_ref.shape
    width, voc = head_ref.shape
    half = tok // 2
    quart = half // 2
    group = 4 * half
    trow = tea_ref.shape[0]
    i, j = lax.axis_index("dp"), lax.axis_index("vocab")
    z, c = j // 2, j % 2
    sib = z * 2 + (1 - c)
    nx = i + 1 - 2 * (i % 2)
    ny = (i + 2) % 4
    nd = 3 - i
    rel = (i, nx, ny, nd)
    to_x, to_y, to_d = {"dp": nx}, {"dp": ny}, {"dp": nd}
    to_rel = (None, to_x, to_y, to_d)
    to_sib = {"vocab": sib}

    def remote(src, dst, ssem, rsem, to):
        return pltpu.make_async_remote_copy(
            src_ref=src, dst_ref=dst, send_sem=ssem, recv_sem=rsem,
            device_id=to, device_id_type=MESH,
        )

    def cut(block, begin=0, size=None):
        size = half if size is None else size
        return pl.ds(pl.multiple_of(block * half + begin, 16), size)

    def rows(h, block, begin=0, size=None):
        return cut(h * 4 + block, begin, size)

    mine = pl.ds(pl.multiple_of(c * feat, feat), feat)
    other = pl.ds(pl.multiple_of((1 - c) * feat, feat), feat)

    own_cols = pl.ds(pl.multiple_of(j * voc, voc), voc)
    own_trow = pl.ds(pl.multiple_of(j * trow, trow), trow)
    cp_hid = pltpu.make_async_copy(hid_ref, zbuf.at[z], loc_sem.at[0])
    cp_head = pltpu.make_async_copy(head_ref, head_v, loc_sem.at[1])
    cp_tea = pltpu.make_async_copy(tea_ref.at[:, own_cols], tea_v.at[own_trow, :], loc_sem.at[2])
    cp_ids = pltpu.make_async_copy(ids_ref, ids_v, loc_sem.at[3])
    cp_mask = pltpu.make_async_copy(mask_ref, mask_v, loc_sem.at[4])
    for cp in (cp_hid, cp_head, cp_tea, cp_ids, cp_mask):
        cp.start()

    barrier = pltpu.get_barrier_semaphore()
    for k in range(1, 4):
        pl.semaphore_signal(barrier, inc=1, device_id={"dp": (i + k) % 4}, device_id_type=MESH)
    for k in range(1, 8):
        pl.semaphore_signal(barrier, inc=1, device_id={"vocab": (j + k) % 8}, device_id_type=MESH)
    pl.semaphore_wait(barrier, 10)

    a1 = ([], [])

    def send_a1(h):
        piece = pl.ds(h * half, half)
        for k in range(1, 4):
            cp = remote(
                hid_ref.at[piece, :], zbuf.at[z, piece, :], a1s.at[h, k], a1r.at[h, k],
                {"vocab": ((z + k) % 4) * 2 + c},
            )
            cp.start()
            a1[h].append(cp)

    def a2_copy(h, zs, shift):
        return remote(
            zbuf.at[zs, pl.ds(h * half, half), :], hblk.at[rows(h, i), mine],
            a2s.at[h, shift], a2r.at[h, shift], {"dp": zs},
        )

    def a2_local(h, zs):
        return pltpu.make_async_copy(
            zbuf.at[zs, pl.ds(h * half, half), :], hblk.at[rows(h, i), mine], loc_sem.at[5 + h]
        )

    def forward(h, zs):
        shift = (zs - i + 4) % 4

        @pl.when(shift != 0)
        def _():
            a2_copy(h, zs, shift).start()

        @pl.when(shift == 0)
        def _():
            a2_local(h, zs).start()

    def forward_all(h):
        forward(h, z)
        for k in range(1, 4):
            a1[h][k - 1].wait_recv()
            forward(h, (z - k + 4) % 4)

    a3 = ([], [])

    def swap_features(h):
        for k in range(4):
            if k == 0:
                a2_local(h, i).wait()
            else:
                a2_copy(h, (i + k) % 4, k).wait_recv()
            piece = hblk.at[rows(h, (i - k + 4) % 4), mine]
            cp = remote(piece, piece, a3s.at[h, k], a3r.at[h, k], to_sib)
            cp.start()
            a3[h].append(cp)
        for cp in a3[h]:
            cp.wait_recv()

    def partial_logits(h):
        x = hblk[pl.ds(h * group, group), :]

        @pl.loop(0, voc // 256)
        def _(t):
            col = pl.ds(pl.multiple_of(t * 256, 256), 256)
            part[h, :, col] = jnp.dot(x, head_v[:, col], preferred_element_type=F32)

    lo, hi = pl.ds(0, quart), pl.ds(quart, quart)
    b = ([], [])

    def send_b(h, src, dst, to):
        n = len(b[h])
        cp = remote(src, dst, bs.at[h, n], br.at[h, n], to)
        cp.start()
        b[h].append(cp)

    def p_lo(h, block):
        return part.at[h, cut(block, 0, quart), :]

    def p_hi(h, block):
        return part.at[h, cut(block, quart, quart), :]

    def sum_start(h):
        send_b(h, p_lo(h, nd), relay.at[h, 0], to_x)
        send_b(h, p_hi(h, nd), relay.at[h, 1], to_y)
        send_b(h, p_lo(h, nx), got.at[h, 0, lo, :], to_x)
        send_b(h, p_hi(h, ny), got.at[h, 1, hi, :], to_y)

    def sum_relay(h):
        b[h][0].wait_recv()
        p_lo(h, ny)[...] = p_lo(h, ny)[...] + relay[h, 0]
        send_b(h, p_lo(h, ny), got.at[h, 1, lo, :], to_y)
        b[h][1].wait_recv()
        p_hi(h, nx)[...] = p_hi(h, nx)[...] + relay[h, 1]
        send_b(h, p_hi(h, nx), got.at[h, 0, hi, :], to_x)

    def teacher_rows(h):
        return tea_v[pl.ds(h * half, half), :].astype(F32)

    st = ([], [])

    def stats_start(h):
        for n in (2, 3, 4, 5):
            b[h][n].wait_recv()
        logits = part[h, cut(i), :] + got[h, 0] + got[h, 1]
        logits_v[h] = logits
        m = jnp.max(logits, axis=1, keepdims=True)
        e = jnp.exp(logits - m)
        s = jnp.sum(e, axis=1, keepdims=True)
        w = jnp.sum(e * (logits - teacher_rows(h)), axis=1, keepdims=True)
        lane = lax.broadcasted_iota(jnp.int32, (half, tok), 1)
        packed = jnp.where(lane == 0, m, jnp.where(lane == 1, s, w))
        packed = jnp.concatenate([packed, packed], axis=0)
        stat_v[h, j] = jnp.swapaxes(packed, 0, 1)[0:8, :]
        for k in range(1, 8):
            cp = remote(
                stat_v.at[h, j], stat_v.at[h, j], ss.at[h, k], sr.at[h, k],
                {"vocab": (j + k) % 8},
            )
            cp.start()
            st[h].append(cp)

    def gradient(h):
        for cp in st[h]:
            cp.wait_recv()
        stats = stat_v[h]
        tops = stats[:, 0, :]
        top = jnp.max(tops, axis=0, keepdims=True)
        scale = jnp.exp(tops - top)
        total = jnp.sum(stats[:, 1, :] * scale, axis=0, keepdims=True)
        weighted = jnp.sum(stats[:, 2, :] * scale, axis=0, keepdims=True)
        sub = lax.broadcasted_iota(jnp.int32, (tok, tok), 0)
        table = jnp.where(sub == 0, top, jnp.where(sub == 1, total, jnp.where(
            sub == 2, weighted / total, jnp.where(
                sub == 3, ids_v[...].astype(F32), mask_v[...].astype(F32)))))
        table = jnp.swapaxes(table, 0, 1)[h * half:(h + 1) * half, :]
        logits = logits_v[h]
        prob = jnp.exp(logits - table[:, 0:1]) / table[:, 1:2]
        gap = logits - teacher_rows(h)
        ids = table[:, 3:4].astype(jnp.int32) - j * voc
        onehot = (lax.broadcasted_iota(jnp.int32, (half, voc), 1) == ids).astype(F32)
        lg = table[:, 4:5] * (prob * (gap - table[:, 2:3]) + anchor_weight * (prob - onehot))
        lgb[rows(h, i), :] = lg.astype(BF16)

    cc = ([], [])

    def send_c(h, block, begin, to):
        n = len(cc[h])
        piece = lgb.at[rows(h, block, begin, quart), :]
        cp = remote(piece, piece, cs.at[h, n], cr.at[h, n], to)
        cp.start()
        cc[h].append(cp)

    def gather_start(h):
        send_c(h, i, 0, to_x)
        send_c(h, i, quart, to_y)
        send_c(h, i, quart, to_x)
        send_c(h, i, 0, to_y)
        cp = pltpu.make_async_copy(
            lgb.at[rows(h, i), :], lg_out.at[pl.ds(h * half, half), :], wsem.at[4 + h])
        cp.start()
        return cp

    def gather_relay(h):
        cc[h][0].wait_recv()
        send_c(h, nx, 0, to_y)
        cc[h][1].wait_recv()
        send_c(h, ny, quart, to_x)

    ecps = []

    def hidden_part(h):
        for n in (2, 3, 4, 5):
            cc[h][n].wait_recv()
        g = lgb[pl.ds(h * group, group), :]
        sib_out[h] = jnp.dot(g, head_t[:, other], preferred_element_type=F32).astype(BF16)
        cp = remote(sib_out.at[h], sib_in.at[h], es.at[h], er.at[h], to_sib)
        cp.start()
        ecps.append(cp)
        hown[h] = jnp.dot(g, head_t[:, mine], preferred_element_type=F32)

    def d2_copy(h, r, shift, zt):
        return remote(
            d1_in.at[h, r], d2_in.at[h, shift], d2s.at[h, shift], d2r.at[h, shift],
            {"vocab": zt * 2 + c},
        )

    def d2_send(h, r):
        zt = rel[r]
        shift = (zt - z + 4) % 4

        @pl.when(shift != 0)
        def _():
            d2_copy(h, r, shift, zt).start()

        @pl.when(shift == 0)
        def _():
            d2_in[h, 0] = d1_in[h, r]

    d1 = ([], [])

    def scatter_start(h):
        ecps[h].wait_recv()
        d1_out[h] = (hown[h] + sib_in[h].astype(F32)).astype(BF16)
        for r in (3, 1, 2):
            cp = remote(
                d1_out.at[h, cut(rel[r]), :], d1_in.at[h, r], d1s.at[h, r], d1r.at[h, r], to_rel[r])
            cp.start()
            d1[h].append(cp)
        d1_in[h, 0] = d1_out[h, cut(i), :]
        d2_send(h, 0)

    def scatter_relay(h):
        for n, r in ((1, 1), (2, 2), (0, 3)):
            d1[h][n].wait_recv()
            d2_send(h, r)

    def scatter_end(h):
        for k in range(1, 4):
            d2_copy(h, 0, k, (z + k) % 4).wait_recv()
        acc = d2_in[h, 0].astype(F32)
        for k in range(1, 4):
            acc = acc + d2_in[h, k].astype(F32)
        hg_v[pl.ds(h * half, half), :] = acc
        piece = pl.ds(h * half, half)
        cp = pltpu.make_async_copy(hg_v.at[piece, :], hg_out.at[piece, :], wsem.at[6 + h])
        cp.start()
        return cp

    wcps = []
    quarter = width // 4

    def weight_part(t):
        band = pl.ds(t * quarter, quarter)

        @pl.loop(0, voc // 256)
        def _(u):
            col = pl.ds(pl.multiple_of(u * 256, 256), 256)
            wg_v[band, col] = jnp.dot(
                hid_t[band, :], lgb[:, col], preferred_element_type=F32).astype(BF16)

        cp = pltpu.make_async_copy(wg_v.at[band, :], wg_out.at[band, :], wsem.at[t])
        cp.start()
        wcps.append(cp)

    send_a1(0)
    cp_hid.wait()
    for cp in a1[0]:
        cp.wait_send()
    send_a1(1)
    forward_all(0)
    swap_features(0)
    cp_head.wait()
    partial_logits(0)
    sum_start(0)
    forward_all(1)
    tcps = []
    for k in range(1, 8):
        jt = (j + k) % 8
        cp = remote(
            tea_ref.at[:, pl.ds(pl.multiple_of(jt * voc, voc), voc)], tea_v.at[own_trow, :],
            ts.at[k], tr.at[k], {"vocab": jt},
        )
        cp.start()
        tcps.append(cp)
    sum_relay(0)
    swap_features(1)
    partial_logits(1)
    sum_start(1)

    @pl.loop(0, width // 256)
    def _(t):
        band = pl.ds(pl.multiple_of(t * 256, 256), 256)
        hid_t[band, :] = jnp.swapaxes(hblk[:, band], 0, 1)

    cp_tea.wait()
    for cp in tcps:
        cp.wait_recv()
    cp_ids.wait()
    cp_mask.wait()
    stats_start(0)
    sum_relay(1)
    gradient(0)
    out_cps = [gather_start(0)]

    @pl.loop(0, width // 256)
    def _(t):
        band = pl.ds(pl.multiple_of(t * 256, 256), 256)
        head_t[:, band] = jnp.swapaxes(head_v[band, :], 0, 1)

    stats_start(1)
    gather_relay(0)
    gradient(1)
    out_cps.append(gather_start(1))
    hidden_part(0)
    gather_relay(1)
    scatter_start(0)
    hidden_part(1)
    scatter_relay(0)
    scatter_start(1)
    weight_part(0)
    weight_part(1)
    scatter_relay(1)
    weight_part(2)
    weight_part(3)
    out_cps.append(scatter_end(0))
    out_cps.append(scatter_end(1))

    for cp in a1[1] + tcps + ecps:
        cp.wait_send()
    for h in range(2):
        for cp in a3[h] + b[h] + st[h] + cc[h] + d1[h]:
            cp.wait_send()
        for k in range(1, 4):
            a2_copy(h, (i + k) % 4, k).wait_send()
            d2_copy(h, 0, k, (z + k) % 4).wait_send()
    for cp in wcps + out_cps:
        cp.wait()


def fused(hidden_states, teacher_logprob, head_weight, token_ids, padding_mask):
    tok, feat = hidden_states.shape
    width, voc = head_weight.shape
    trow = teacher_logprob.shape[0]
    half = tok // 2
    any_spec = pl.BlockSpec(memory_space=pl.ANY)
    dma = pltpu.SemaphoreType.DMA
    return pl.pallas_call(
        kernel,
        out_shape=(
            jax.ShapeDtypeStruct((tok, voc), BF16),
            jax.ShapeDtypeStruct((tok, feat), F32),
            jax.ShapeDtypeStruct((width, voc), BF16),
        ),
        in_specs=[any_spec] * 5,
        out_specs=[any_spec] * 3,
        scratch_shapes=[
            pltpu.VMEM((width, voc), BF16),
            pltpu.VMEM((voc, width), BF16),
            pltpu.VMEM((4, tok, feat), BF16),
            pltpu.VMEM((4 * tok, width), BF16),
            pltpu.VMEM((width, 4 * tok), BF16),
            pltpu.VMEM((8 * trow, voc), BF16),
            pltpu.VMEM((1, tok), jnp.int32),
            pltpu.VMEM((1, tok), jnp.int32),
            pltpu.VMEM((2, 4 * half, voc), F32),
            pltpu.VMEM((2, 2, half // 2, voc), F32),
            pltpu.VMEM((2, 2, half, voc), F32),
            pltpu.VMEM((2, half, voc), F32),
            pltpu.VMEM((2, 8, 8, tok), F32),
            pltpu.VMEM((4 * tok, voc), BF16),
            pltpu.VMEM((2, 4 * half, feat), F32),
            pltpu.VMEM((2, 4 * half, feat), BF16),
            pltpu.VMEM((2, 4 * half, feat), BF16),
            pltpu.VMEM((2, 4 * half, feat), BF16),
            pltpu.VMEM((2, 4, half, feat), BF16),
            pltpu.VMEM((2, 4, half, feat), BF16),
            pltpu.VMEM((width, voc), BF16),
            pltpu.VMEM((tok, feat), F32),
            dma((7,)), dma((2, 4)), dma((2, 4)), dma((2, 4)), dma((2, 4)), dma((2, 4)), dma((2, 4)),
            dma((8,)), dma((8,)), dma((2, 6)), dma((2, 6)), dma((2, 8)), dma((2, 8)),
            dma((2, 6)), dma((2, 6)), dma((2,)), dma((2,)), dma((2, 4)), dma((2, 4)),
            dma((2, 4)), dma((2, 4)), dma((8,)),
        ],
        compiler_params=pltpu.CompilerParams(
            collective_id=0, has_side_effects=True, vmem_limit_bytes=62 * 1024 * 1024
        ),
        cost_estimate=pl.CostEstimate(
            flops=6 * 4 * tok * width * voc, bytes_accessed=6 * width * voc,
            transcendentals=2 * tok * voc,
        ),
    )(
        hidden_states, teacher_logprob, head_weight,
        token_ids.reshape(1, tok), padding_mask.reshape(1, tok),
    )


def gathered(n_dp, n_vocab, hidden_states, teacher_logprob, head_weight, token_ids, padding_mask):
    voc = head_weight.shape[1]
    full = lax.all_gather(hidden_states, "vocab", axis=1, tiled=True)
    block = lax.all_to_all(full, "dp", split_axis=1, concat_axis=0, tiled=True)
    teacher = lax.all_to_all(teacher_logprob, "vocab", split_axis=1, concat_axis=0, tiled=True)
    part = jnp.dot(block, head_weight, preferred_element_type=F32)
    logits = lax.psum_scatter(part, "dp", scatter_dimension=0, tiled=True)
    gap = logits - teacher.astype(F32)
    top = lax.pmax(jnp.max(logits, axis=1), "vocab")
    expo = jnp.exp(logits - top[:, None])
    total, weighted = lax.psum((jnp.sum(expo, axis=1), jnp.sum(expo * gap, axis=1)), "vocab")
    columns = lax.axis_index("vocab") * voc + jnp.arange(voc, dtype=jnp.int32)
    onehot = (columns[None, :] == token_ids[:, None]).astype(F32)
    prob = expo / total[:, None]
    keep = padding_mask.astype(F32)[:, None]
    logit_grad = (
        keep * (prob * (gap - (weighted / total)[:, None]) + anchor_weight * (prob - onehot))
    ).astype(BF16)
    every = lax.all_gather(logit_grad, "dp", axis=0, tiled=True)
    head_grad = lax.dot_general(
        block, every, (((0,), (0,)), ((), ())), preferred_element_type=F32).astype(BF16)
    back = lax.dot_general(
        every, head_weight, (((1,), (1,)), ((), ())), preferred_element_type=F32)
    back = lax.all_to_all(back, "dp", split_axis=0, concat_axis=1, tiled=True)
    hidden_grad = lax.psum_scatter(back, "vocab", scatter_dimension=1, tiled=True)
    return (logit_grad, hidden_grad, head_grad)


def solution(mesh):
    in_specs = (P("dp", "vocab"), P(("dp", "vocab"), None), P("dp", "vocab"), P("dp"), P("dp"))
    out_specs = (P("dp", "vocab"), P("dp", "vocab"), P("dp", "vocab"))
    n_dp, n_vocab = mesh.shape["dp"], mesh.shape["vocab"]
    body = fused if (n_dp, n_vocab) == (4, 8) else functools.partial(gathered, n_dp, n_vocab)
    return jax.shard_map(body, mesh=mesh, in_specs=in_specs, out_specs=out_specs, check_vma=False)
```

time: 239 us -> 79.2 us (0.33)
  waiting for transfers between devices: 146 us -> 0 us
  Pallas kernels: 0 us -> 72 us
  blocking collectives: 48.4 us -> 0 us
  matrix products: 15.3 us -> 0 us
  between operations: 13.8 us -> 0.64 us
  starting transfers between devices: 5.04 us -> 0 us
    all_gather x3 -> x0, waiting for transfers between devices: 112 us -> none  [the longest x1 88.7 us: local(): head_full = lax.all_gather(head_weight, 'dp', axis=0, tiled=True)]
    pallas_call x0 -> x1, Pallas kernels: none -> 72 us  [fused(): pl.pallas_call(kernel, out_shape=(jax.ShapeDtypeStruct((tok, voc), BF16),...]
    reduce_scatter x1 -> x0, waiting for transfers between devices: 32.9 us -> none  [local(): lax.psum_scatter(feature_part, 'vocab', scatter_dimension=1, tiled=True)]
    all_to_all x1 -> x0, blocking collectives: 18.3 us -> none  [local(): lax.all_to_all(hidden_full, 'dp', split_axis=1, concat_axis=0, tiled=True)]
    pmax x1 -> x0, blocking collectives: 16.5 us -> none  [local(): top = lax.pmax(jnp.max(logits, axis=1), 'vocab')]
    dot_general x3 -> x0, matrix products: 15.3 us -> none  [the longest x1 7.71 us: local(): lax.dot_general(logit_grad, head_full, (((1,), (1,)), ((), ())), preferre...]
    psum x1 -> x0, blocking collectives: 13.6 us -> none  [local(): lax.psum((jnp.sum(expo, axis=1), jnp.sum(expo * gap, axis=1)), 'vocab')]
    all_to_all x1 -> x0, starting transfers between devices: 4.88 us -> none  [local(): lax.all_to_all(teacher_logprob, 'vocab', split_axis=1, concat_axis=0, til...]
  transfers between devices with their start and end apart: 5 -> 0, of which waited for: 4 -> 0; matrix products, arithmetic and copies ran while one was open for 9% -> 0% of each run, Pallas kernels for 0% -> 0%
where the time goes in v2:
time: 79.2 us; the launch traced here: 79 us
  Pallas kernels  72 us (91%)
  local copies, waits for them, and re-layouts  6.42 us (8%)
    pallas_call x1, Pallas kernels, fused(): pl.pallas_call(kernel, out_shape=(jax.ShapeDtypeStruct((tok, voc), BF16),...  72 us
    unnamed x3, local copies, waits for them, and re-layouts  6.42 us

profile of v2, /device:TPU:6, one launch (start us, length us, event | category | flops | bytes accessed | tf_op | source)
XLA Modules:
  0.0 79.0 jit_solution(10860545276001015383)
XLA Ops:
  0.6 72.0 %shard_map.76 = (bf16[128,1024]{1,0:T(8,128)(2,1)}, f32[128,512]{1,0:T(8,128)}, bf16[1024,1024]{1,0:T(8,128)(2,1)}) custom-call(bf16[128,512]{1,0:T(8,128)(2,1)} %hid_ref.1, bf16[16,8192]{1,0:T(8,128)(2,1)} %tea_ref.1, bf16[1024,1024]{1,0:T(8,128)(2,1)} %head_ref.1, s32[1,128]{1,0:T(1,128)} %bitcast.2, s32[1,128]{1,0:T(1,128)} %bitcast.3), custom_call_target="tpu_custom_call" | custom-call | flops 3221225472 | bytes 6291456 | tf_op jit(solution)/shard_map/pallas_call | solution.py:396
  72.6 1.7 %copy.11 = bf16[128,1024]{1,0:T(8,128)(2,1)} copy(bf16[128,1024]{1,0:T(8,128)(2,1)} %get-tuple-element.6) | data formatting | bytes 524288
  74.3 1.7 %copy.12 = f32[128,512]{1,0:T(8,128)} copy(f32[128,512]{1,0:T(8,128)} %get-tuple-element.7) | data formatting | bytes 524288
  75.9 3.1 %copy.13 = bf16[1024,1024]{1,0:T(8,128)(2,1)} copy(bf16[1024,1024]{1,0:T(8,128)(2,1)} %get-tuple-element.8) | data formatting | bytes 4194304

commit v3 on v2

--- a/solution.py
+++ b/solution.py
@@ -104,15 +104,14 @@
         def _():
             a2_local(h, zs).start()
 
-    def forward_all(h):
-        forward(h, z)
+    def forward_rest(h):
         for k in range(1, 4):
             a1[h][k - 1].wait_recv()
             forward(h, (z - k + 4) % 4)
 
     a3 = ([], [])
 
-    def swap_features(h):
+    def swap_start(h):
         for k in range(4):
             if k == 0:
                 a2_local(h, i).wait()
@@ -122,6 +121,8 @@
             cp = remote(piece, piece, a3s.at[h, k], a3r.at[h, k], to_sib)
             cp.start()
             a3[h].append(cp)
+
+    def swap_end(h):
         for cp in a3[h]:
             cp.wait_recv()
 
@@ -311,17 +312,35 @@
         cp.start()
         wcps.append(cp)
 
+    def turn_head(t):
+        band = pl.ds(t * quarter, quarter)
+        head_t[:, band] = jnp.swapaxes(head_v[band, :], 0, 1)
+
+    def turn_hidden(h):
+        group_rows = pl.ds(h * group, group)
+
+        @pl.loop(0, width // 256)
+        def _(t):
+            band = pl.ds(pl.multiple_of(t * 256, 256), 256)
+            hid_t[band, group_rows] = jnp.swapaxes(hblk[group_rows, band], 0, 1)
+
     send_a1(0)
     cp_hid.wait()
+    forward(0, z)
     for cp in a1[0]:
         cp.wait_send()
     send_a1(1)
-    forward_all(0)
-    swap_features(0)
     cp_head.wait()
+    turn_head(0)
+    forward_rest(0)
+    turn_head(1)
+    swap_start(0)
+    turn_head(2)
+    swap_end(0)
     partial_logits(0)
     sum_start(0)
-    forward_all(1)
+    forward(1, z)
+    forward_rest(1)
     tcps = []
     for k in range(1, 8):
         jt = (j + k) % 8
@@ -331,33 +350,25 @@
         )
         cp.start()
         tcps.append(cp)
+    turn_head(3)
     sum_relay(0)
-    swap_features(1)
+    swap_start(1)
+    swap_end(1)
     partial_logits(1)
     sum_start(1)
-
-    @pl.loop(0, width // 256)
-    def _(t):
-        band = pl.ds(pl.multiple_of(t * 256, 256), 256)
-        hid_t[band, :] = jnp.swapaxes(hblk[:, band], 0, 1)
-
     cp_tea.wait()
     for cp in tcps:
         cp.wait_recv()
     cp_ids.wait()
     cp_mask.wait()
     stats_start(0)
+    turn_hidden(0)
+    gradient(0)
     sum_relay(1)
-    gradient(0)
     out_cps = [gather_start(0)]
-
-    @pl.loop(0, width // 256)
-    def _(t):
-        band = pl.ds(pl.multiple_of(t * 256, 256), 256)
-        head_t[:, band] = jnp.swapaxes(head_v[band, :], 0, 1)
-
+    turn_hidden(1)
+    gather_relay(0)
     stats_start(1)
-    gather_relay(0)
     gradient(1)
     out_cps.append(gather_start(1))
     hidden_part(0)
@@ -386,6 +397,21 @@
         cp.wait()
 
 
+def store(lg_ref, hg_ref, wg_ref, lg_out, hg_out, wg_out, sem):
+    copies = [
+        pltpu.make_async_copy(lg_ref, lg_out, sem.at[4]),
+        pltpu.make_async_copy(hg_ref, hg_out, sem.at[5]),
+    ]
+    quarter = wg_ref.shape[0] // 4
+    for t in range(4):
+        band = pl.ds(t * quarter, quarter)
+        copies.append(pltpu.make_async_copy(wg_ref.at[band, :], wg_out.at[band, :], sem.at[t]))
+    for cp in copies:
+        cp.start()
+    for cp in copies:
+        cp.wait()
+
+
 def fused(hidden_states, teacher_logprob, head_weight, token_ids, padding_mask):
     tok, feat = hidden_states.shape
     width, voc = head_weight.shape
@@ -393,14 +419,14 @@
     half = tok // 2
     any_spec = pl.BlockSpec(memory_space=pl.ANY)
     dma = pltpu.SemaphoreType.DMA
-    return pl.pallas_call(
+    held = pl.pallas_call(
         kernel,
         out_shape=(
             jax.ShapeDtypeStruct((tok, voc), BF16),
             jax.ShapeDtypeStruct((tok, feat), F32),
             jax.ShapeDtypeStruct((width, voc), BF16),
         ),
-        in_specs=[any_spec] * 5,
+        in_specs=[pl.BlockSpec(memory_space=pltpu.HBM)] * 5,
         out_specs=[any_spec] * 3,
         scratch_shapes=[
             pltpu.VMEM((width, voc), BF16),
@@ -441,6 +467,14 @@
         hidden_states, teacher_logprob, head_weight,
         token_ids.reshape(1, tok), padding_mask.reshape(1, tok),
     )
+    return pl.pallas_call(
+        store,
+        out_shape=tuple(jax.ShapeDtypeStruct(x.shape, x.dtype) for x in held),
+        in_specs=[any_spec] * 3,
+        out_specs=[pl.BlockSpec(memory_space=pltpu.HBM)] * 3,
+        scratch_shapes=[dma((6,))],
+        compiler_params=pltpu.CompilerParams(vmem_limit_bytes=62 * 1024 * 1024),
+    )(*held)
 
 
 def gathered(n_dp, n_vocab, hidden_states, teacher_logprob, head_weight, token_ids, padding_mask):

time: 79.2 us -> 155 us (1.96)
  Pallas kernels: 72 us -> 154 us
  local copies, waits for them, and re-layouts: 6.42 us -> 0 us
    pallas_call x0 -> x1, Pallas kernels: none -> 80.6 us  [fused(): pl.pallas_call(store, out_shape=tuple((jax.ShapeDtypeStruct(x.shape, x.dt...]
    unnamed x3 -> x0, local copies, waits for them, and re-layouts: 6.42 us -> none
where the time goes in v3:
time: 155 us
  Pallas kernels  154 us (99%)
    pallas_call x1, Pallas kernels, fused(): pl.pallas_call(store, out_shape=tuple((jax.ShapeDtypeStruct(x.shape, x.dt...  80.6 us
    pallas_call x1, Pallas kernels, fused(): pl.pallas_call(kernel, out_shape=(jax.ShapeDtypeStruct((tok, voc), BF16),...  73.4 us

profile of v3, /device:TPU:6, one launch (start us, length us, event | category | flops | bytes accessed | tf_op | source)
XLA Modules:
  0.0 154.6 jit_solution(15107003432670937558)
XLA Ops:
  0.6 73.4 %shard_map.76 = (bf16[128,1024]{1,0:T(8,128)(2,1)}, f32[128,512]{1,0:T(8,128)}, bf16[1024,1024]{1,0:T(8,128)(2,1)}) custom-call(bf16[128,512]{1,0:T(8,128)(2,1)} %hid_ref.1, bf16[16,8192]{1,0:T(8,128)(2,1)} %tea_ref.1, bf16[1024,1024]{1,0:T(8,128)(2,1)} %head_ref.1, s32[1,128]{1,0:T(1,128)} %bitcast.2, s32[1,128]{1,0:T(1,128)} %bitcast.3), custom_call_target="tpu_custom_call" | custom-call | flops 3221225472 | bytes 6291456 | tf_op jit(solution)/shard_map/pallas_call | solution.py:422
  74.0 80.6 %shard_map.77 = (bf16[128,1024]{1,0:T(8,128)(2,1)}, f32[128,512]{1,0:T(8,128)}, bf16[1024,1024]{1,0:T(8,128)(2,1)}) custom-call(bf16[128,1024]{1,0:T(8,128)(2,1)} %get-tuple-element.6.lg_ref, f32[128,512]{1,0:T(8,128)} %get-tuple-element.7.hg_ref, bf16[1024,1024]{1,0:T(8,128)(2,1)} %get-tuple-element.8.wg_ref), custom_call_target="tpu_custom_call" | custom-call | tf_op jit(solution)/shard_map/pallas_call | solution.py:470

commit v4 on v3

--- a/solution.py
+++ b/solution.py
@@ -15,7 +15,7 @@
 def kernel(
     hid_ref, tea_ref, head_ref, ids_ref, mask_ref,
     lg_out, hg_out, wg_out,
-    head_v, head_t, zbuf, hblk, hid_t, tea_v, ids_v, mask_v, part, relay, got, logits_v, stat_v,
+    head_v, head_t, zbuf, hblk, hid_t, tea_src, tea_v, ids_v, mask_v, part, relay, got, logits_v, stat_v,
     lgb, hown, sib_out, sib_in, d1_out, d1_in, d2_in, wg_v, hg_v,
     loc_sem, a1s, a1r, a2s, a2r, a3s, a3r, ts, tr, bs, br, ss, sr, cs, cr,
     es, er, d1s, d1r, d2s, d2r, wsem,
@@ -57,7 +57,7 @@
     own_trow = pl.ds(pl.multiple_of(j * trow, trow), trow)
     cp_hid = pltpu.make_async_copy(hid_ref, zbuf.at[z], loc_sem.at[0])
     cp_head = pltpu.make_async_copy(head_ref, head_v, loc_sem.at[1])
-    cp_tea = pltpu.make_async_copy(tea_ref.at[:, own_cols], tea_v.at[own_trow, :], loc_sem.at[2])
+    cp_tea = pltpu.make_async_copy(tea_ref, tea_src, loc_sem.at[2])
     cp_ids = pltpu.make_async_copy(ids_ref, ids_v, loc_sem.at[3])
     cp_mask = pltpu.make_async_copy(mask_ref, mask_v, loc_sem.at[4])
     for cp in (cp_hid, cp_head, cp_tea, cp_ids, cp_mask):
@@ -76,7 +76,7 @@
         piece = pl.ds(h * half, half)
         for k in range(1, 4):
             cp = remote(
-                hid_ref.at[piece, :], zbuf.at[z, piece, :], a1s.at[h, k], a1r.at[h, k],
+                zbuf.at[z, piece, :], zbuf.at[z, piece, :], a1s.at[h, k], a1r.at[h, k],
                 {"vocab": ((z + k) % 4) * 2 + c},
             )
             cp.start()
@@ -88,11 +88,6 @@
             a2s.at[h, shift], a2r.at[h, shift], {"dp": zs},
         )
 
-    def a2_local(h, zs):
-        return pltpu.make_async_copy(
-            zbuf.at[zs, pl.ds(h * half, half), :], hblk.at[rows(h, i), mine], loc_sem.at[5 + h]
-        )
-
     def forward(h, zs):
         shift = (zs - i + 4) % 4
 
@@ -102,7 +97,7 @@
 
         @pl.when(shift == 0)
         def _():
-            a2_local(h, zs).start()
+            hblk[rows(h, i), mine] = zbuf[zs, pl.ds(h * half, half), :]
 
     def forward_rest(h):
         for k in range(1, 4):
@@ -113,9 +108,7 @@
 
     def swap_start(h):
         for k in range(4):
-            if k == 0:
-                a2_local(h, i).wait()
-            else:
+            if k > 0:
                 a2_copy(h, (i + k) % 4, k).wait_recv()
             piece = hblk.at[rows(h, (i - k + 4) % 4), mine]
             cp = remote(piece, piece, a3s.at[h, k], a3r.at[h, k], to_sib)
@@ -324,8 +317,8 @@
             band = pl.ds(pl.multiple_of(t * 256, 256), 256)
             hid_t[band, group_rows] = jnp.swapaxes(hblk[group_rows, band], 0, 1)
 
+    cp_hid.wait()
     send_a1(0)
-    cp_hid.wait()
     forward(0, z)
     for cp in a1[0]:
         cp.wait_send()
@@ -341,11 +334,13 @@
     sum_start(0)
     forward(1, z)
     forward_rest(1)
+    cp_tea.wait()
+    tea_v[own_trow, :] = tea_src[:, own_cols]
     tcps = []
     for k in range(1, 8):
         jt = (j + k) % 8
         cp = remote(
-            tea_ref.at[:, pl.ds(pl.multiple_of(jt * voc, voc), voc)], tea_v.at[own_trow, :],
+            tea_src.at[:, pl.ds(pl.multiple_of(jt * voc, voc), voc)], tea_v.at[own_trow, :],
             ts.at[k], tr.at[k], {"vocab": jt},
         )
         cp.start()
@@ -356,7 +351,6 @@
     swap_end(1)
     partial_logits(1)
     sum_start(1)
-    cp_tea.wait()
     for cp in tcps:
         cp.wait_recv()
     cp_ids.wait()
@@ -397,18 +391,19 @@
         cp.wait()
 
 
-def store(lg_ref, hg_ref, wg_ref, lg_out, hg_out, wg_out, sem):
-    copies = [
-        pltpu.make_async_copy(lg_ref, lg_out, sem.at[4]),
-        pltpu.make_async_copy(hg_ref, hg_out, sem.at[5]),
-    ]
+def store(lg_ref, hg_ref, wg_ref, lg_out, hg_out, wg_out, lg_v, hg_v, wg_v, load_sem, store_sem):
     quarter = wg_ref.shape[0] // 4
-    for t in range(4):
-        band = pl.ds(t * quarter, quarter)
-        copies.append(pltpu.make_async_copy(wg_ref.at[band, :], wg_out.at[band, :], sem.at[t]))
-    for cp in copies:
-        cp.start()
-    for cp in copies:
+    steps = [(wg_ref.at[pl.ds(t * quarter, quarter), :], wg_v.at[pl.ds(t * quarter, quarter), :],
+              wg_out.at[pl.ds(t * quarter, quarter), :]) for t in range(4)]
+    steps += [(lg_ref, lg_v, lg_out), (hg_ref, hg_v, hg_out)]
+    loads = [pltpu.make_async_copy(a, v, load_sem.at[n]) for n, (a, v, o) in enumerate(steps)]
+    stores = [pltpu.make_async_copy(v, o, store_sem.at[n]) for n, (a, v, o) in enumerate(steps)]
+    for cp in loads:
+        cp.start()
+    for load, save in zip(loads, stores):
+        load.wait()
+        save.start()
+    for cp in stores:
         cp.wait()
 
 
@@ -434,6 +429,7 @@
             pltpu.VMEM((4, tok, feat), BF16),
             pltpu.VMEM((4 * tok, width), BF16),
             pltpu.VMEM((width, 4 * tok), BF16),
+            pltpu.VMEM(teacher_logprob.shape, BF16),
             pltpu.VMEM((8 * trow, voc), BF16),
             pltpu.VMEM((1, tok), jnp.int32),
             pltpu.VMEM((1, tok), jnp.int32),
@@ -451,7 +447,7 @@
             pltpu.VMEM((2, 4, half, feat), BF16),
             pltpu.VMEM((width, voc), BF16),
             pltpu.VMEM((tok, feat), F32),
-            dma((7,)), dma((2, 4)), dma((2, 4)), dma((2, 4)), dma((2, 4)), dma((2, 4)), dma((2, 4)),
+            dma((5,)), dma((2, 4)), dma((2, 4)), dma((2, 4)), dma((2, 4)), dma((2, 4)), dma((2, 4)),
             dma((8,)), dma((8,)), dma((2, 6)), dma((2, 6)), dma((2, 8)), dma((2, 8)),
             dma((2, 6)), dma((2, 6)), dma((2,)), dma((2,)), dma((2, 4)), dma((2, 4)),
             dma((2, 4)), dma((2, 4)), dma((8,)),
@@ -472,7 +468,7 @@
         out_shape=tuple(jax.ShapeDtypeStruct(x.shape, x.dtype) for x in held),
         in_specs=[any_spec] * 3,
         out_specs=[pl.BlockSpec(memory_space=pltpu.HBM)] * 3,
-        scratch_shapes=[dma((6,))],
+        scratch_shapes=[pltpu.VMEM(x.shape, x.dtype) for x in held] + [dma((6,)), dma((6,))],
         compiler_params=pltpu.CompilerParams(vmem_limit_bytes=62 * 1024 * 1024),
     )(*held)
 

time: 155 us -> 76.6 us (0.49)
  Pallas kernels: 154 us -> 75.8 us
    pallas_call x1, Pallas kernels: 80.6 us -> 2.63 us  [fused(): pl.pallas_call(store, out_shape=tuple((jax.ShapeDtypeStruct(x.shape, x.dt...]
where the time goes in v4:
time: 76.6 us; the launch traced here: 76.5 us
  Pallas kernels  75.8 us (99%)
    pallas_call x1, Pallas kernels, fused(): pl.pallas_call(kernel, out_shape=(jax.ShapeDtypeStruct((tok, voc), BF16),...  73.2 us
    pallas_call x1, Pallas kernels, fused(): pl.pallas_call(store, out_shape=tuple((jax.ShapeDtypeStruct(x.shape, x.dt...  2.63 us

profile of v4, /device:TPU:6, one launch (start us, length us, event | category | flops | bytes accessed | tf_op | source)
XLA Modules:
  0.0 76.5 jit_solution(13282388600112005098)
XLA Ops:
  0.6 73.2 %shard_map.76 = (bf16[128,1024]{1,0:T(8,128)(2,1)}, f32[128,512]{1,0:T(8,128)}, bf16[1024,1024]{1,0:T(8,128)(2,1)}) custom-call(bf16[128,512]{1,0:T(8,128)(2,1)} %hid_ref.1, bf16[16,8192]{1,0:T(8,128)(2,1)} %tea_ref.1, bf16[1024,1024]{1,0:T(8,128)(2,1)} %head_ref.1, s32[1,128]{1,0:T(1,128)} %bitcast.2, s32[1,128]{1,0:T(1,128)} %bitcast.3), custom_call_target="tpu_custom_call" | custom-call | flops 3221225472 | bytes 6291456 | tf_op jit(solution)/shard_map/pallas_call | solution.py:417
  73.8 2.6 %shard_map.77 = (bf16[128,1024]{1,0:T(8,128)(2,1)}, f32[128,512]{1,0:T(8,128)}, bf16[1024,1024]{1,0:T(8,128)(2,1)}) custom-call(bf16[128,1024]{1,0:T(8,128)(2,1)} %get-tuple-element.6.lg_ref, f32[128,512]{1,0:T(8,128)} %get-tuple-element.7.hg_ref, bf16[1024,1024]{1,0:T(8,128)(2,1)} %get-tuple-element.8.wg_ref), custom_call_target="tpu_custom_call" | custom-call | tf_op jit(solution)/shard_map/pallas_call | solution.py:466

commit v5 on v4

--- a/solution.py
+++ b/solution.py
@@ -22,7 +22,7 @@
 ):
     tok, feat = hid_ref.shape
     width, voc = head_ref.shape
-    half = tok // 2
+    half = tok // 4
     quart = half // 2
     group = 4 * half
     trow = tea_ref.shape[0]
@@ -70,7 +70,7 @@
         pl.semaphore_signal(barrier, inc=1, device_id={"vocab": (j + k) % 8}, device_id_type=MESH)
     pl.semaphore_wait(barrier, 10)
 
-    a1 = ([], [])
+    a1 = ([], [], [], [])
 
     def send_a1(h):
         piece = pl.ds(h * half, half)
@@ -104,7 +104,7 @@
             a1[h][k - 1].wait_recv()
             forward(h, (z - k + 4) % 4)
 
-    a3 = ([], [])
+    a3 = ([], [], [], [])
 
     def swap_start(h):
         for k in range(4):
@@ -128,7 +128,7 @@
             part[h, :, col] = jnp.dot(x, head_v[:, col], preferred_element_type=F32)
 
     lo, hi = pl.ds(0, quart), pl.ds(quart, quart)
-    b = ([], [])
+    b = ([], [], [], [])
 
     def send_b(h, src, dst, to):
         n = len(b[h])
@@ -159,7 +159,7 @@
     def teacher_rows(h):
         return tea_v[pl.ds(h * half, half), :].astype(F32)
 
-    st = ([], [])
+    st = ([], [], [], [])
 
     def stats_start(h):
         for n in (2, 3, 4, 5):
@@ -172,7 +172,7 @@
         w = jnp.sum(e * (logits - teacher_rows(h)), axis=1, keepdims=True)
         lane = lax.broadcasted_iota(jnp.int32, (half, tok), 1)
         packed = jnp.where(lane == 0, m, jnp.where(lane == 1, s, w))
-        packed = jnp.concatenate([packed, packed], axis=0)
+        packed = jnp.concatenate([packed] * 4, axis=0)
         stat_v[h, j] = jnp.swapaxes(packed, 0, 1)[0:8, :]
         for k in range(1, 8):
             cp = remote(
@@ -204,7 +204,7 @@
         lg = table[:, 4:5] * (prob * (gap - table[:, 2:3]) + anchor_weight * (prob - onehot))
         lgb[rows(h, i), :] = lg.astype(BF16)
 
-    cc = ([], [])
+    cc = ([], [], [], [])
 
     def send_c(h, block, begin, to):
         n = len(cc[h])
@@ -259,7 +259,7 @@
         def _():
             d2_in[h, 0] = d1_in[h, r]
 
-    d1 = ([], [])
+    d1 = ([], [], [], [])
 
     def scatter_start(h):
         ecps[h].wait_recv()
@@ -285,7 +285,7 @@
             acc = acc + d2_in[h, k].astype(F32)
         hg_v[pl.ds(h * half, half), :] = acc
         piece = pl.ds(h * half, half)
-        cp = pltpu.make_async_copy(hg_v.at[piece, :], hg_out.at[piece, :], wsem.at[6 + h])
+        cp = pltpu.make_async_copy(hg_v.at[piece, :], hg_out.at[piece, :], wsem.at[8 + h])
         cp.start()
         return cp
 
@@ -316,6 +316,14 @@
         def _(t):
             band = pl.ds(pl.multiple_of(t * 256, 256), 256)
             hid_t[band, group_rows] = jnp.swapaxes(hblk[group_rows, band], 0, 1)
+
+    def logits_start(h):
+        swap_start(h)
+        swap_end(h)
+        partial_logits(h)
+        sum_start(h)
+
+    out_cps = []
 
     cp_hid.wait()
     send_a1(0)
@@ -332,8 +340,10 @@
     swap_end(0)
     partial_logits(0)
     sum_start(0)
+    send_a1(2)
     forward(1, z)
     forward_rest(1)
+    send_a1(3)
     cp_tea.wait()
     tea_v[own_trow, :] = tea_src[:, own_cols]
     tcps = []
@@ -347,41 +357,62 @@
         tcps.append(cp)
     turn_head(3)
     sum_relay(0)
-    swap_start(1)
-    swap_end(1)
-    partial_logits(1)
-    sum_start(1)
+    logits_start(1)
+    forward(2, z)
+    forward_rest(2)
     for cp in tcps:
         cp.wait_recv()
     cp_ids.wait()
     cp_mask.wait()
     stats_start(0)
     turn_hidden(0)
+    sum_relay(1)
     gradient(0)
-    sum_relay(1)
-    out_cps = [gather_start(0)]
+    out_cps.append(gather_start(0))
+    logits_start(2)
+    forward(3, z)
+    forward_rest(3)
+    stats_start(1)
     turn_hidden(1)
     gather_relay(0)
-    stats_start(1)
+    sum_relay(2)
     gradient(1)
     out_cps.append(gather_start(1))
+    logits_start(3)
     hidden_part(0)
+    stats_start(2)
+    turn_hidden(2)
     gather_relay(1)
     scatter_start(0)
+    sum_relay(3)
+    gradient(2)
+    out_cps.append(gather_start(2))
     hidden_part(1)
+    stats_start(3)
+    turn_hidden(3)
+    gather_relay(2)
+    scatter_start(1)
     scatter_relay(0)
-    scatter_start(1)
+    gradient(3)
+    out_cps.append(gather_start(3))
+    hidden_part(2)
+    gather_relay(3)
+    scatter_start(2)
+    scatter_relay(1)
+    hidden_part(3)
+    scatter_relay(2)
+    scatter_start(3)
     weight_part(0)
     weight_part(1)
-    scatter_relay(1)
+    scatter_relay(3)
     weight_part(2)
     weight_part(3)
-    out_cps.append(scatter_end(0))
-    out_cps.append(scatter_end(1))
-
-    for cp in a1[1] + tcps + ecps:
+    for h in range(4):
+        out_cps.append(scatter_end(h))
+
+    for cp in a1[1] + a1[2] + a1[3] + tcps + ecps:
         cp.wait_send()
-    for h in range(2):
+    for h in range(4):
         for cp in a3[h] + b[h] + st[h] + cc[h] + d1[h]:
             cp.wait_send()
         for k in range(1, 4):
@@ -411,7 +442,7 @@
     tok, feat = hidden_states.shape
     width, voc = head_weight.shape
     trow = teacher_logprob.shape[0]
-    half = tok // 2
+    half = tok // 4
     any_spec = pl.BlockSpec(memory_space=pl.ANY)
     dma = pltpu.SemaphoreType.DMA
     held = pl.pallas_call(
@@ -433,24 +464,24 @@
             pltpu.VMEM((8 * trow, voc), BF16),
             pltpu.VMEM((1, tok), jnp.int32),
             pltpu.VMEM((1, tok), jnp.int32),
-            pltpu.VMEM((2, 4 * half, voc), F32),
-            pltpu.VMEM((2, 2, half // 2, voc), F32),
-            pltpu.VMEM((2, 2, half, voc), F32),
-            pltpu.VMEM((2, half, voc), F32),
-            pltpu.VMEM((2, 8, 8, tok), F32),
+            pltpu.VMEM((4, 4 * half, voc), F32),
+            pltpu.VMEM((4, 2, half // 2, voc), F32),
+            pltpu.VMEM((4, 2, half, voc), F32),
+            pltpu.VMEM((4, half, voc), F32),
+            pltpu.VMEM((4, 8, 8, tok), F32),
             pltpu.VMEM((4 * tok, voc), BF16),
-            pltpu.VMEM((2, 4 * half, feat), F32),
-            pltpu.VMEM((2, 4 * half, feat), BF16),
-            pltpu.VMEM((2, 4 * half, feat), BF16),
-            pltpu.VMEM((2, 4 * half, feat), BF16),
-            pltpu.VMEM((2, 4, half, feat), BF16),
-            pltpu.VMEM((2, 4, half, feat), BF16),
+            pltpu.VMEM((4, 4 * half, feat), F32),
+            pltpu.VMEM((4, 4 * half, feat), BF16),
+            pltpu.VMEM((4, 4 * half, feat), BF16),
+            pltpu.VMEM((4, 4 * half, feat), BF16),
+            pltpu.VMEM((4, 4, half, feat), BF16),
+            pltpu.VMEM((4, 4, half, feat), BF16),
             pltpu.VMEM((width, voc), BF16),
             pltpu.VMEM((tok, feat), F32),
-            dma((5,)), dma((2, 4)), dma((2, 4)), dma((2, 4)), dma((2, 4)), dma((2, 4)), dma((2, 4)),
-            dma((8,)), dma((8,)), dma((2, 6)), dma((2, 6)), dma((2, 8)), dma((2, 8)),
-            dma((2, 6)), dma((2, 6)), dma((2,)), dma((2,)), dma((2, 4)), dma((2, 4)),
-            dma((2, 4)), dma((2, 4)), dma((8,)),
+            dma((5,)), dma((4, 4)), dma((4, 4)), dma((4, 4)), dma((4, 4)), dma((4, 4)), dma((4, 4)),
+            dma((8,)), dma((8,)), dma((4, 6)), dma((4, 6)), dma((4, 8)), dma((4, 8)),
+            dma((4, 6)), dma((4, 6)), dma((4,)), dma((4,)), dma((4, 4)), dma((4, 4)),
+            dma((4, 4)), dma((4, 4)), dma((12,)),
         ],
         compiler_params=pltpu.CompilerParams(
             collective_id=0, has_side_effects=True, vmem_limit_bytes=62 * 1024 * 1024

time: 76.6 us -> 77.4 us (1.010)
  Pallas kernels: 75.8 us -> 76.6 us
    pallas_call x1, Pallas kernels: 73.2 us -> 74 us  [fused(): pl.pallas_call(kernel, out_shape=(jax.ShapeDtypeStruct((tok, voc), BF16),...]
where the time goes in v5:
time: 77.4 us; the launch traced here: 77.3 us
  Pallas kernels  76.6 us (99%)
    pallas_call x1, Pallas kernels, fused(): pl.pallas_call(kernel, out_shape=(jax.ShapeDtypeStruct((tok, voc), BF16),...  74 us
    pallas_call x1, Pallas kernels, fused(): pl.pallas_call(store, out_shape=tuple((jax.ShapeDtypeStruct(x.shape, x.dt...  2.63 us

profile of v5, /device:TPU:6, one launch (start us, length us, event | category | flops | bytes accessed | tf_op | source)
XLA Modules:
  0.0 77.3 jit_solution(6712460681453145225)
XLA Ops:
  0.6 74.0 %shard_map.76 = (bf16[128,1024]{1,0:T(8,128)(2,1)}, f32[128,512]{1,0:T(8,128)}, bf16[1024,1024]{1,0:T(8,128)(2,1)}) custom-call(bf16[128,512]{1,0:T(8,128)(2,1)} %hid_ref.1, bf16[16,8192]{1,0:T(8,128)(2,1)} %tea_ref.1, bf16[1024,1024]{1,0:T(8,128)(2,1)} %head_ref.1, s32[1,128]{1,0:T(1,128)} %bitcast.2, s32[1,128]{1,0:T(1,128)} %bitcast.3), custom_call_target="tpu_custom_call" | custom-call | flops 3221225472 | bytes 6291456 | tf_op jit(solution)/shard_map/pallas_call | solution.py:448
  74.7 2.6 %shard_map.77 = (bf16[128,1024]{1,0:T(8,128)(2,1)}, f32[128,512]{1,0:T(8,128)}, bf16[1024,1024]{1,0:T(8,128)(2,1)}) custom-call(bf16[128,1024]{1,0:T(8,128)(2,1)} %get-tuple-element.6.lg_ref, f32[128,512]{1,0:T(8,128)} %get-tuple-element.7.hg_ref, bf16[1024,1024]{1,0:T(8,128)(2,1)} %get-tuple-element.8.wg_ref), custom_call_target="tpu_custom_call" | custom-call | tf_op jit(solution)/shard_map/pallas_call | solution.py:497
